TPU v7x, 32 devices: a whole 2x2x4 slice. The times are simulated.
32 devices in a mesh: st: 4 (over y, x), tp: 8 (over z, core).
Axes of the slice: x: 2, y: 2, z: 4, core: 2. Of those that a mesh axis runs over, the one named last changes fastest.
Arguments:
- continuous: bfloat16 [64, 3, 1424], P(('st', 'tp')), may hold values from -48 to 48
- templates: bfloat16 [64, 12, 3, 400], P(('st', 'tp')), may hold values from -120 to 120
- station_list: int32 [64, 12], P(('st', 'tp')), may hold values from 0 to 63, as said below
- moveouts: int32 [64, 12], P(('st', 'tp')), may hold values from 0 to 256
Outputs:
- detection: float32 [64, 768], P(('st', 'tp'))
Inputs may be any that keep to these rules, and one draw needn't show every extreme that they name: `station_list`: A station's group is station // 16. The 12 stations of a template are distinct, and so are their indices within their groups (station % 16). The rows of one device (2 templates, aligned blocks in order) name at most 12 stations of any one group, and in every such block one group is named exactly 12 times; blocks b and b2 with b % 8 == b2 % 8 share that group.
All inputs are finite; a program needn't handle non-finite values.
Results may differ from a plain program's by a relative error of at most 0.0003.
Values may be sent and summed in bfloat16 or wider, within the bound.
A program may use at most 64 MiB of HBM per device.

v0:
```python
import functools

import jax
import jax.numpy as jnp
from jax import lax
from jax.experimental import pallas as pl
from jax.experimental.pallas import tpu as pltpu
from jax.sharding import PartitionSpec as P

WIN = 768
TLEN = 400
CH = 3
DLEN = 1424
EPS = 1e-05
LANES = 128
ROWS = 16
FRAMES = WIN // LANES
LAG = 32
PHASES = LANES // LAG
STEPS = 4
DEPTH = STEPS * LANES
AHEAD = 4

MESH = pl.DeviceIdType.MESH


def kernel(groups, members, continuous_in, templates_in, stations_in, moveouts_in, out, continuous,
           templates, stations, moveouts, records, bands, scales, padded, shifted, window, load_sem,
           send_sem, recv_sem):
    loads = [
        pltpu.make_async_copy(source, target, load_sem.at[n])
        for n, (source, target) in enumerate(
            [(continuous_in, continuous), (templates_in, templates),
             (stations_in, stations), (moveouts_in, moveouts)])
    ]
    for load in loads:
        load.start()
    own = continuous.shape[1]
    list_size, _, template_count = templates.shape[:3]
    depth_count = members // 2
    st = lax.axis_index("st")
    tp = lax.axis_index("tp")
    z = tp // 2
    core = tp % 2

    def block(group, member):
        return group * members + member

    def rows(index):
        return records.at[pl.ds(index * own, own)]

    def copy(index, send, group, member):
        return pltpu.make_async_remote_copy(
            src_ref=rows(index),
            dst_ref=rows(index),
            send_sem=send_sem.at[send],
            recv_sem=recv_sem.at[index],
            device_id=(group, member),
            device_id_type=MESH,
        )

    def z_peer(step):
        return lax.rem(z + step, depth_count)

    def group_peer(step):
        return lax.rem(st + step, groups)

    partner = z * 2 + 1 - core

    barrier = pltpu.get_barrier_semaphore()
    for step in range(1, depth_count):
        pl.semaphore_signal(barrier, 1, device_id=(st, z_peer(step) * 2 + core), device_id_type=MESH)
    for step in range(1, groups):
        pl.semaphore_signal(barrier, 1, device_id=(group_peer(step), tp), device_id_type=MESH)
    pl.semaphore_signal(barrier, 1, device_id=(st, partner), device_id_type=MESH)

    loads[0].wait()

    me = block(st, tp)
    full = DLEN // LANES
    for c in range(CH):
        record = continuous[c].astype(jnp.float32)
        for s in range(own):
            pieces = [record[s : s + 1, n * LANES : (n + 1) * LANES] for n in range(full)]
            tail = jnp.concatenate(
                [record[s : s + 1, full * LANES :],
                 jnp.zeros((1, LANES - (DLEN - full * LANES)), jnp.float32)], axis=1)
            pieces.append(tail)
            pieces.append(jnp.zeros((ROWS - full - 1, LANES), jnp.float32))
            records[me * own + s, c * ROWS : (c + 1) * ROWS, :] = jnp.concatenate(
                pieces, axis=0
            ).astype(jnp.bfloat16)

    pl.semaphore_wait(barrier, depth_count - 1 + groups - 1 + 1)

    xy_base = depth_count - 1
    core_base = xy_base + depth_count * (groups - 1)
    sends = []

    def start(descriptor):
        descriptor.start()
        sends.append(descriptor)

    def to_groups(index, z_step):
        for step in range(1, groups):
            start(copy(index, xy_base + z_step * (groups - 1) + step - 1, group_peer(step), tp))

    def to_partner(index, place):
        start(copy(index, core_base + place, st, partner))

    for step in range(1, depth_count):
        start(copy(me, step - 1, st, z_peer(step) * 2 + core))
    to_groups(me, 0)
    to_partner(me, 0)

    loads[1].wait()

    padded[...] = jnp.zeros_like(padded)

    def build(k):
        for c in range(CH):
            padded[k, c, :, :TLEN] = templates[k, c].astype(jnp.float32)
            wave = padded[k, c]
            energy = jnp.sum(wave * wave, axis=1, keepdims=True)
            scale = lax.rsqrt(energy / TLEN + EPS) / TLEN
            scales[k, c] = jnp.broadcast_to(scale, (template_count, LANES))
            for t in range(template_count):
                spread = jnp.broadcast_to(wave[t : t + 1], (LAG, DEPTH))
                bands[k, t, c * LAG : (c + 1) * LAG, :] = pltpu.roll(
                    spread, 0, 1, stride=1, stride_axis=0
                ).astype(jnp.bfloat16)
        for t in range(template_count):
            bands[k, t, CH * LAG :, :] = jnp.zeros((LANES - CH * LAG, DEPTH), jnp.bfloat16)

    def build_range(first, last):
        def body(k, carry):
            build(k)
            return carry

        lax.fori_loop(first, last, body, 0)

    third = list_size // 3
    build_range(0, third)

    def arrived(index):
        copy(index, 0, st, tp).wait_recv()

    for step in range(1, depth_count):
        source = block(st, lax.rem(z + depth_count - step, depth_count) * 2 + core)
        arrived(source)
        to_groups(source, step)
        to_partner(source, step)
    build_range(third, 2 * third)
    place = depth_count
    for step in range(1, groups):
        group = lax.rem(st + groups - step, groups)
        for z_step in range(depth_count):
            source = block(group, lax.rem(z + depth_count - z_step, depth_count) * 2 + core)
            arrived(source)
            to_partner(source, place)
            place += 1
    build_range(2 * third, list_size)

    reach = (STEPS + 1) * LANES
    row_at = lax.broadcasted_iota(jnp.int32, (reach, LANES), 0)
    lane_at = lax.broadcasted_iota(jnp.int32, (reach, LANES), 1)
    inside = jnp.logical_and(row_at >= lane_at, row_at < lane_at + TLEN)
    window[...] = jnp.where(inside, 1.0, 0.0).astype(jnp.bfloat16)

    for group_step in range(groups):
        for z_step in range(depth_count):
            source = block(lax.rem(st + group_step, groups),
                           lax.rem(z + z_step, depth_count) * 2 + 1 - core)
            arrived(source)

    loads[2].wait()
    loads[3].wait()
    lane = lax.broadcasted_iota(jnp.int32, (8, LANES), 1)

    def shift_into(slot, t, k):
        record = records[stations[t, k]].astype(jnp.float32)
        for phase in range(PHASES):
            skip = lax.rem(moveouts[t, k] + phase * LAG, LANES)
            shifted[slot, phase] = pltpu.roll(record, lax.rem(LANES - skip, LANES), 1)

    def frames(slot, t, k, phase, c, count):
        shift = moveouts[t, k] + phase * LAG
        first = c * ROWS + lax.div(shift, LANES)
        pieces = [shifted[slot, phase, pl.ds(first + n, 8), :] for n in range(count + 1)]
        here = lane < LANES - lax.rem(shift, LANES)
        return [jnp.where(here, pieces[n], pieces[n + 1]) for n in range(count)]

    def gather(slot, t, k):
        left, high, low = [], [], []
        for c in range(CH):
            for phase in range(PHASES):
                parts = frames(slot, t, k, phase, c, STEPS + 1 if phase == 0 else STEPS)
                left.append(jnp.concatenate(parts[:STEPS], axis=1))
                if phase == 0:
                    square = [part * part for part in parts]
                    rounded = [part.astype(jnp.bfloat16).astype(jnp.float32) for part in square]
                    high.append(jnp.concatenate(rounded, axis=1))
                    low.append(
                        jnp.concatenate([v - r for v, r in zip(square, rounded)], axis=1))
        raw = lax.dot_general(
            jnp.concatenate(left, axis=0).astype(jnp.bfloat16), bands[k, t],
            (((1,), (1,)), ((), ())), preferred_element_type=jnp.float32)
        return raw, jnp.concatenate(high + low, axis=0).astype(jnp.bfloat16)

    def finish(raw, sums, t, k):
        total = jnp.zeros((8, LANES), jnp.float32)
        for c in range(CH):
            energy = sums[c * 8 : (c + 1) * 8] + sums[(CH + c) * 8 : (CH + c + 1) * 8]
            level = lax.rsqrt(energy / TLEN + EPS)
            lags = None
            for phase in range(PHASES):
                at = (c * PHASES + phase) * 8
                piece = raw[at : at + 8]
                if phase != c:
                    piece = pltpu.roll(piece, (phase - c) % PHASES * LAG, 1)
                lags = piece if phase == 0 else jnp.where(lane < phase * LAG, lags, piece)
            total = total + lags * level * scales[k, c, t : t + 1, :]
        return total

    def work(step, totals):
        totals = list(totals)
        batch = [(t, step * AHEAD + ahead) for ahead in range(AHEAD) for t in range(template_count)]
        for slot, (t, k) in enumerate(batch):
            shift_into(slot, t, k)
        gathered = [gather(slot, t, k) for slot, (t, k) in enumerate(batch)]
        sums = jnp.dot(
            jnp.concatenate([squares for _, squares in gathered], axis=0), window[...],
            preferred_element_type=jnp.float32)
        each = 2 * CH * 8
        for slot, (t, k) in enumerate(batch):
            totals[t] = totals[t] + finish(
                gathered[slot][0], sums[slot * each : (slot + 1) * each], t, k)
        return tuple(totals)

    totals = lax.fori_loop(
        0, list_size // AHEAD, work,
        tuple(jnp.zeros((8, LANES), jnp.float32) for _ in range(template_count)))
    for t in range(template_count):
        for n in range(FRAMES):
            out[t : t + 1, n * LANES : (n + 1) * LANES] = totals[t][n : n + 1]
    for descriptor in sends:
        descriptor.wait_send()


def shards(groups, members, continuous, templates, station_list, moveouts):
    own = continuous.shape[0]
    template_count, list_size = templates.shape[:2]
    depth_count = members // 2
    send_count = depth_count - 1 + depth_count * (groups - 1) + depth_count * groups
    waves = continuous.transpose(1, 0, 2)
    shapes = templates.transpose(1, 2, 0, 3)
    entries = template_count * list_size * CH
    return pl.pallas_call(
        functools.partial(kernel, groups, members),
        out_shape=jax.ShapeDtypeStruct((template_count, WIN), jnp.float32),
        in_specs=[pl.BlockSpec(memory_space=pltpu.HBM)] * 4,
        out_specs=pl.BlockSpec(memory_space=pltpu.VMEM),
        scratch_shapes=[
            pltpu.VMEM(waves.shape, waves.dtype),
            pltpu.VMEM(shapes.shape, shapes.dtype),
            pltpu.SMEM(station_list.shape, jnp.int32),
            pltpu.SMEM(moveouts.shape, jnp.int32),
            pltpu.VMEM((groups * members * own, CH * ROWS, LANES), jnp.bfloat16),
            pltpu.VMEM((list_size, template_count, LANES, DEPTH), jnp.bfloat16),
            pltpu.VMEM((list_size, CH, template_count, LANES), jnp.float32),
            pltpu.VMEM((list_size, CH, template_count, DEPTH), jnp.float32),
            pltpu.VMEM((AHEAD * template_count, PHASES, CH * ROWS, LANES), jnp.float32),
            pltpu.VMEM(((STEPS + 1) * LANES, LANES), jnp.bfloat16),
            pltpu.SemaphoreType.DMA((4,)),
            pltpu.SemaphoreType.DMA((send_count,)),
            pltpu.SemaphoreType.DMA((groups * members,)),
        ],
        compiler_params=pltpu.CompilerParams(
            collective_id=0, has_side_effects=True, vmem_limit_bytes=64 * 2**20
        ),
        cost_estimate=pl.CostEstimate(
            flops=entries * 2 * 8 * DEPTH * LANES, bytes_accessed=2**20, transcendentals=entries * 2048
        ),
    )(waves, shapes, station_list, moveouts)


def solution(mesh):
    placed = (
        P(("st", "tp"), None, None),
        P(("st", "tp"), None, None, None),
        P(("st", "tp"), None),
        P(("st", "tp"), None),
    )
    return jax.shard_map(
        functools.partial(shards, mesh.shape["st"], mesh.shape["tp"]),
        mesh=mesh, in_specs=placed, out_specs=P(("st", "tp"), None), check_vma=False
    )
```

profile of v0, /device:TPU:1, one launch (start us, length us, event | category | flops | bytes accessed | tf_op | source)
XLA Modules:
  0.0 19.2 jit_solution(2749222403345094637)
XLA Ops:
  0.0 17.9 %shard_map.46 = f32[2,768]{1,0:T(2,128)} custom-call(bf16[3,2,1424]{2,1,0:T(2,128)(2,1)} %bitcast.3, bf16[12,3,2,400]{3,2,1,0:T(2,128)(2,1)} %bitcast.2, s32[2,12]{1,0:T(2,128)} %stations_in.1, s32[2,12]{1,0:T(2,128)} %moveouts_in.1), custom_call_target="tpu_custom_call" | custom-call | flops 75497472 | bytes 1048576 | tf_op jit(solution)/shard_map/pallas_call | solution.py:258
  17.9 1.3 %copy.6 = f32[2,768]{1,0:T(2,128)} copy(f32[2,768]{1,0:T(2,128)} %shard_map.46) | data formatting | bytes 12288
where the time goes:
time: 19.4 us; the launch traced here: 19.2 us
  Pallas kernels  17.9 us (92%)
  local copies, waits for them, and re-layouts  1.29 us (7%)
    pallas_call x1, Pallas kernels, shards(): pl.pallas_call(functools.partial(kernel, groups, members), out_shape=jax....  17.9 us
    unnamed x1, local copies, waits for them, and re-layouts  1.29 us

commit v1 on v0

--- a/solution.py
+++ b/solution.py
@@ -13,7 +13,8 @@
 DLEN = 1424
 EPS = 1e-05
 LANES = 128
-ROWS = 16
+ROWS = 12
+STATION = 40
 FRAMES = WIN // LANES
 LAG = 32
 PHASES = LANES // LAG
@@ -47,7 +48,7 @@
         return group * members + member
 
     def rows(index):
-        return records.at[pl.ds(index * own, own)]
+        return records.at[index]
 
     def copy(index, send, group, member):
         return pltpu.make_async_remote_copy(
@@ -65,33 +66,43 @@
     def group_peer(step):
         return lax.rem(st + step, groups)
 
+    square_group = groups == 4
+    if square_group:
+        along_x = st + 1 - 2 * lax.rem(st, 2)
+        along_y = lax.rem(st + 2, 4)
+        first = along_x + core * (along_y - along_x)
+        second = along_y + core * (along_x - along_y)
+        direct = [second, first]
+    else:
+        direct = [group_peer(step) for step in range(1, groups)]
+
     partner = z * 2 + 1 - core
 
     barrier = pltpu.get_barrier_semaphore()
     for step in range(1, depth_count):
         pl.semaphore_signal(barrier, 1, device_id=(st, z_peer(step) * 2 + core), device_id_type=MESH)
-    for step in range(1, groups):
-        pl.semaphore_signal(barrier, 1, device_id=(group_peer(step), tp), device_id_type=MESH)
+    for group in direct:
+        pl.semaphore_signal(barrier, 1, device_id=(group, tp), device_id_type=MESH)
     pl.semaphore_signal(barrier, 1, device_id=(st, partner), device_id_type=MESH)
 
     loads[0].wait()
 
     me = block(st, tp)
     full = DLEN // LANES
-    for c in range(CH):
-        record = continuous[c].astype(jnp.float32)
-        for s in range(own):
-            pieces = [record[s : s + 1, n * LANES : (n + 1) * LANES] for n in range(full)]
-            tail = jnp.concatenate(
-                [record[s : s + 1, full * LANES :],
-                 jnp.zeros((1, LANES - (DLEN - full * LANES)), jnp.float32)], axis=1)
-            pieces.append(tail)
-            pieces.append(jnp.zeros((ROWS - full - 1, LANES), jnp.float32))
-            records[me * own + s, c * ROWS : (c + 1) * ROWS, :] = jnp.concatenate(
-                pieces, axis=0
-            ).astype(jnp.bfloat16)
-
-    pl.semaphore_wait(barrier, depth_count - 1 + groups - 1 + 1)
+    pieces = []
+    for s in range(own):
+        for c in range(CH):
+            record = continuous[c].astype(jnp.float32)[s : s + 1]
+            pieces += [record[:, n * LANES : (n + 1) * LANES] for n in range(full)]
+            pieces.append(jnp.concatenate(
+                [record[:, full * LANES :],
+                 jnp.zeros((1, LANES - (DLEN - full * LANES)), jnp.float32)], axis=1))
+        pieces.append(jnp.zeros((STATION - CH * ROWS, LANES), jnp.float32))
+    if records.shape[1] > own * STATION:
+        pieces.append(jnp.zeros((records.shape[1] - own * STATION, LANES), jnp.float32))
+    records[me] = jnp.concatenate(pieces, axis=0).astype(jnp.bfloat16)
+
+    pl.semaphore_wait(barrier, depth_count - 1 + len(direct) + 1)
 
     xy_base = depth_count - 1
     core_base = xy_base + depth_count * (groups - 1)
@@ -102,8 +113,11 @@
         sends.append(descriptor)
 
     def to_groups(index, z_step):
-        for step in range(1, groups):
-            start(copy(index, xy_base + z_step * (groups - 1) + step - 1, group_peer(step), tp))
+        for place, group in enumerate(direct):
+            start(copy(index, xy_base + z_step * (groups - 1) + place, group, tp))
+
+    def forward(index, z_step):
+        start(copy(index, xy_base + z_step * (groups - 1) + 2, first, tp))
 
     def to_partner(index, place):
         start(copy(index, core_base + place, st, partner))
@@ -118,19 +132,23 @@
     padded[...] = jnp.zeros_like(padded)
 
     def build(k):
+        waves = []
         for c in range(CH):
             padded[k, c, :, :TLEN] = templates[k, c].astype(jnp.float32)
             wave = padded[k, c]
             energy = jnp.sum(wave * wave, axis=1, keepdims=True)
             scale = lax.rsqrt(energy / TLEN + EPS) / TLEN
             scales[k, c] = jnp.broadcast_to(scale, (template_count, LANES))
-            for t in range(template_count):
-                spread = jnp.broadcast_to(wave[t : t + 1], (LAG, DEPTH))
-                bands[k, t, c * LAG : (c + 1) * LAG, :] = pltpu.roll(
-                    spread, 0, 1, stride=1, stride_axis=0
-                ).astype(jnp.bfloat16)
+            waves.append(wave)
         for t in range(template_count):
-            bands[k, t, CH * LAG :, :] = jnp.zeros((LANES - CH * LAG, DEPTH), jnp.bfloat16)
+            turned = [
+                pltpu.roll(
+                    jnp.broadcast_to(wave[t : t + 1], (LAG, DEPTH)), 0, 1, stride=1, stride_axis=0
+                )
+                for wave in waves
+            ]
+            turned.append(jnp.zeros((LANES - CH * LAG, DEPTH), jnp.float32))
+            bands[k, t] = jnp.concatenate(turned, axis=0).T.astype(jnp.bfloat16)
 
     def build_range(first, last):
         def body(k, carry):
@@ -139,27 +157,36 @@
 
         lax.fori_loop(first, last, body, 0)
 
-    third = list_size // 3
-    build_range(0, third)
+    def quarter(n):
+        build_range(n * list_size // 4, (n + 1) * list_size // 4)
 
     def arrived(index):
         copy(index, 0, st, tp).wait_recv()
 
+    def from_z(group, step):
+        return block(group, lax.rem(z + depth_count - step, depth_count) * 2 + core)
+
+    quarter(0)
     for step in range(1, depth_count):
-        source = block(st, lax.rem(z + depth_count - step, depth_count) * 2 + core)
+        source = from_z(st, step)
         arrived(source)
         to_groups(source, step)
         to_partner(source, step)
-    build_range(third, 2 * third)
+    quarter(1)
     place = depth_count
-    for step in range(1, groups):
-        group = lax.rem(st + groups - step, groups)
-        for z_step in range(depth_count):
-            source = block(group, lax.rem(z + depth_count - z_step, depth_count) * 2 + core)
+    others = [second, first, 3 - st] if square_group else [
+        lax.rem(st + groups - step, groups) for step in range(1, groups)]
+    for number, group in enumerate(others):
+        for step in range(depth_count):
+            source = from_z(group, step)
             arrived(source)
+            if square_group and number == 0:
+                forward(source, step)
             to_partner(source, place)
             place += 1
-    build_range(2 * third, list_size)
+        if number == 0:
+            quarter(2)
+    quarter(3)
 
     reach = (STEPS + 1) * LANES
     row_at = lax.broadcasted_iota(jnp.int32, (reach, LANES), 0)
@@ -178,7 +205,12 @@
     lane = lax.broadcasted_iota(jnp.int32, (8, LANES), 1)
 
     def shift_into(slot, t, k):
-        record = records[stations[t, k]].astype(jnp.float32)
+        station = stations[t, k]
+        held = records[lax.div(station, own)].astype(jnp.float32)
+        record = held[:STATION]
+        for s in range(1, own):
+            record = jnp.where(
+                lax.rem(station, own) == s, held[s * STATION : (s + 1) * STATION], record)
         for phase in range(PHASES):
             skip = lax.rem(moveouts[t, k] + phase * LAG, LANES)
             shifted[slot, phase] = pltpu.roll(record, lax.rem(LANES - skip, LANES), 1)
@@ -204,7 +236,7 @@
                         jnp.concatenate([v - r for v, r in zip(square, rounded)], axis=1))
         raw = lax.dot_general(
             jnp.concatenate(left, axis=0).astype(jnp.bfloat16), bands[k, t],
-            (((1,), (1,)), ((), ())), preferred_element_type=jnp.float32)
+            (((1,), (0,)), ((), ())), preferred_element_type=jnp.float32)
         return raw, jnp.concatenate(high + low, axis=0).astype(jnp.bfloat16)
 
     def finish(raw, sums, t, k):
@@ -265,11 +297,11 @@
             pltpu.VMEM(shapes.shape, shapes.dtype),
             pltpu.SMEM(station_list.shape, jnp.int32),
             pltpu.SMEM(moveouts.shape, jnp.int32),
-            pltpu.VMEM((groups * members * own, CH * ROWS, LANES), jnp.bfloat16),
-            pltpu.VMEM((list_size, template_count, LANES, DEPTH), jnp.bfloat16),
+            pltpu.VMEM((groups * members, -(-own * STATION // 16) * 16, LANES), jnp.bfloat16),
+            pltpu.VMEM((list_size, template_count, DEPTH, LANES), jnp.bfloat16),
             pltpu.VMEM((list_size, CH, template_count, LANES), jnp.float32),
             pltpu.VMEM((list_size, CH, template_count, DEPTH), jnp.float32),
-            pltpu.VMEM((AHEAD * template_count, PHASES, CH * ROWS, LANES), jnp.float32),
+            pltpu.VMEM((AHEAD * template_count, PHASES, STATION, LANES), jnp.float32),
             pltpu.VMEM(((STEPS + 1) * LANES, LANES), jnp.bfloat16),
             pltpu.SemaphoreType.DMA((4,)),
             pltpu.SemaphoreType.DMA((send_count,)),

time: 19.4 us -> 21.3 us (1.098)
  Pallas kernels: 17.9 us -> 19.8 us
    pallas_call x1, Pallas kernels: 17.9 us -> 19.8 us  [shards(): pl.pallas_call(functools.partial(kernel, groups, members), out_shape=jax....]
where the time goes in v1:
time: 21.3 us; the launch traced here: 21.1 us
  Pallas kernels  19.8 us (93%)
  local copies, waits for them, and re-layouts  1.29 us (6%)
    pallas_call x1, Pallas kernels, shards(): pl.pallas_call(functools.partial(kernel, groups, members), out_shape=jax....  19.8 us
    unnamed x1, local copies, waits for them, and re-layouts  1.29 us

profile of v1, /device:TPU:1, one launch (start us, length us, event | category | flops | bytes accessed | tf_op | source)
XLA Modules:
  0.0 21.1 jit_solution(14420996099440732445)
XLA Ops:
  0.0 19.8 %shard_map.46 = f32[2,768]{1,0:T(2,128)} custom-call(bf16[3,2,1424]{2,1,0:T(2,128)(2,1)} %bitcast.3, bf16[12,3,2,400]{3,2,1,0:T(2,128)(2,1)} %bitcast.2, s32[2,12]{1,0:T(2,128)} %stations_in.1, s32[2,12]{1,0:T(2,128)} %moveouts_in.1), custom_call_target="tpu_custom_call" | custom-call | flops 75497472 | bytes 1048576 | tf_op jit(solution)/shard_map/pallas_call | solution.py:290
  19.8 1.3 %copy.6 = f32[2,768]{1,0:T(2,128)} copy(f32[2,768]{1,0:T(2,128)} %shard_map.46) | data formatting | bytes 12288

commit v2 on v1

--- a/solution.py
+++ b/solution.py
@@ -20,7 +20,7 @@
 PHASES = LANES // LAG
 STEPS = 4
 DEPTH = STEPS * LANES
-AHEAD = 4
+AHEAD = 6
 
 MESH = pl.DeviceIdType.MESH
 
@@ -66,16 +66,10 @@
     def group_peer(step):
         return lax.rem(st + step, groups)
 
-    square_group = groups == 4
-    if square_group:
-        along_x = st + 1 - 2 * lax.rem(st, 2)
-        along_y = lax.rem(st + 2, 4)
-        first = along_x + core * (along_y - along_x)
-        second = along_y + core * (along_x - along_y)
-        direct = [second, first]
+    if groups == 4:
+        direct = [st + 1 - 2 * lax.rem(st, 2), lax.rem(st + 2, 4), 3 - st]
     else:
         direct = [group_peer(step) for step in range(1, groups)]
-
     partner = z * 2 + 1 - core
 
     barrier = pltpu.get_barrier_semaphore()
@@ -116,9 +110,6 @@
         for place, group in enumerate(direct):
             start(copy(index, xy_base + z_step * (groups - 1) + place, group, tp))
 
-    def forward(index, z_step):
-        start(copy(index, xy_base + z_step * (groups - 1) + 2, first, tp))
-
     def to_partner(index, place):
         start(copy(index, core_base + place, st, partner))
 
@@ -141,14 +132,11 @@
             scales[k, c] = jnp.broadcast_to(scale, (template_count, LANES))
             waves.append(wave)
         for t in range(template_count):
-            turned = [
-                pltpu.roll(
+            for c, wave in enumerate(waves):
+                bands[k, t, c * LAG : (c + 1) * LAG, :] = pltpu.roll(
                     jnp.broadcast_to(wave[t : t + 1], (LAG, DEPTH)), 0, 1, stride=1, stride_axis=0
-                )
-                for wave in waves
-            ]
-            turned.append(jnp.zeros((LANES - CH * LAG, DEPTH), jnp.float32))
-            bands[k, t] = jnp.concatenate(turned, axis=0).T.astype(jnp.bfloat16)
+                ).astype(jnp.bfloat16)
+            bands[k, t, CH * LAG :, :] = jnp.zeros((LANES - CH * LAG, DEPTH), jnp.bfloat16)
 
     def build_range(first, last):
         def body(k, carry):
@@ -157,8 +145,10 @@
 
         lax.fori_loop(first, last, body, 0)
 
+    cuts = [0, list_size // 6, list_size // 2, 3 * list_size // 4, list_size]
+
     def quarter(n):
-        build_range(n * list_size // 4, (n + 1) * list_size // 4)
+        build_range(cuts[n], cuts[n + 1])
 
     def arrived(index):
         copy(index, 0, st, tp).wait_recv()
@@ -174,14 +164,10 @@
         to_partner(source, step)
     quarter(1)
     place = depth_count
-    others = [second, first, 3 - st] if square_group else [
-        lax.rem(st + groups - step, groups) for step in range(1, groups)]
-    for number, group in enumerate(others):
+    for number, group in enumerate(direct):
         for step in range(depth_count):
             source = from_z(group, step)
             arrived(source)
-            if square_group and number == 0:
-                forward(source, step)
             to_partner(source, place)
             place += 1
         if number == 0:
@@ -236,14 +222,9 @@
                         jnp.concatenate([v - r for v, r in zip(square, rounded)], axis=1))
         raw = lax.dot_general(
             jnp.concatenate(left, axis=0).astype(jnp.bfloat16), bands[k, t],
-            (((1,), (0,)), ((), ())), preferred_element_type=jnp.float32)
-        return raw, jnp.concatenate(high + low, axis=0).astype(jnp.bfloat16)
-
-    def finish(raw, sums, t, k):
-        total = jnp.zeros((8, LANES), jnp.float32)
-        for c in range(CH):
-            energy = sums[c * 8 : (c + 1) * 8] + sums[(CH + c) * 8 : (CH + c + 1) * 8]
-            level = lax.rsqrt(energy / TLEN + EPS)
+            (((1,), (1,)), ((), ())), preferred_element_type=jnp.float32)
+        merged = []
+        for c in range(CH):
             lags = None
             for phase in range(PHASES):
                 at = (c * PHASES + phase) * 8
@@ -251,7 +232,14 @@
                 if phase != c:
                     piece = pltpu.roll(piece, (phase - c) % PHASES * LAG, 1)
                 lags = piece if phase == 0 else jnp.where(lane < phase * LAG, lags, piece)
-            total = total + lags * level * scales[k, c, t : t + 1, :]
+            merged.append(lags * scales[k, c, t : t + 1, :])
+        return merged, jnp.concatenate(high + low, axis=0).astype(jnp.bfloat16)
+
+    def finish(merged, sums):
+        total = jnp.zeros((8, LANES), jnp.float32)
+        for c in range(CH):
+            energy = sums[c * 8 : (c + 1) * 8] + sums[(CH + c) * 8 : (CH + c + 1) * 8]
+            total = total + merged[c] * lax.rsqrt(energy / TLEN + EPS)
         return total
 
     def work(step, totals):
@@ -266,7 +254,7 @@
         each = 2 * CH * 8
         for slot, (t, k) in enumerate(batch):
             totals[t] = totals[t] + finish(
-                gathered[slot][0], sums[slot * each : (slot + 1) * each], t, k)
+                gathered[slot][0], sums[slot * each : (slot + 1) * each])
         return tuple(totals)
 
     totals = lax.fori_loop(
@@ -298,7 +286,7 @@
             pltpu.SMEM(station_list.shape, jnp.int32),
             pltpu.SMEM(moveouts.shape, jnp.int32),
             pltpu.VMEM((groups * members, -(-own * STATION // 16) * 16, LANES), jnp.bfloat16),
-            pltpu.VMEM((list_size, template_count, DEPTH, LANES), jnp.bfloat16),
+            pltpu.VMEM((list_size, template_count, LANES, DEPTH), jnp.bfloat16),
             pltpu.VMEM((list_size, CH, template_count, LANES), jnp.float32),
             pltpu.VMEM((list_size, CH, template_count, DEPTH), jnp.float32),
             pltpu.VMEM((AHEAD * template_count, PHASES, STATION, LANES), jnp.float32),

time: 21.3 us -> 19.1 us (0.90)
  Pallas kernels: 19.8 us -> 17.6 us
    pallas_call x1, Pallas kernels: 19.8 us -> 17.6 us  [shards(): pl.pallas_call(functools.partial(kernel, groups, members), out_shape=jax....]
where the time goes in v2:
time: 19.1 us; the launch traced here: 18.9 us
  Pallas kernels  17.6 us (92%)
  local copies, waits for them, and re-layouts  1.29 us (7%)
    pallas_call x1, Pallas kernels, shards(): pl.pallas_call(functools.partial(kernel, groups, members), out_shape=jax....  17.6 us
    unnamed x1, local copies, waits for them, and re-layouts  1.29 us

profile of v2, /device:TPU:1, one launch (start us, length us, event | category | flops | bytes accessed | tf_op | source)
XLA Modules:
  0.0 18.9 jit_solution(16165551254397590086)
XLA Ops:
  0.0 17.6 %shard_map.46 = f32[2,768]{1,0:T(2,128)} custom-call(bf16[3,2,1424]{2,1,0:T(2,128)(2,1)} %bitcast.3, bf16[12,3,2,400]{3,2,1,0:T(2,128)(2,1)} %bitcast.2, s32[2,12]{1,0:T(2,128)} %stations_in.1, s32[2,12]{1,0:T(2,128)} %moveouts_in.1), custom_call_target="tpu_custom_call" | custom-call | flops 75497472 | bytes 1048576 | tf_op jit(solution)/shard_map/pallas_call | solution.py:278
  17.6 1.3 %copy.6 = f32[2,768]{1,0:T(2,128)} copy(f32[2,768]{1,0:T(2,128)} %shard_map.46) | data formatting | bytes 12288

commit v3 on v2

--- a/solution.py
+++ b/solution.py
@@ -277,7 +277,7 @@
     entries = template_count * list_size * CH
     return pl.pallas_call(
         functools.partial(kernel, groups, members),
-        out_shape=jax.ShapeDtypeStruct((template_count, WIN), jnp.float32),
+        out_shape=pltpu.VMEM((template_count, WIN), jnp.float32),
         in_specs=[pl.BlockSpec(memory_space=pltpu.HBM)] * 4,
         out_specs=pl.BlockSpec(memory_space=pltpu.VMEM),
         scratch_shapes=[
@@ -296,12 +296,12 @@
             pltpu.SemaphoreType.DMA((groups * members,)),
         ],
         compiler_params=pltpu.CompilerParams(
-            collective_id=0, has_side_effects=True, vmem_limit_bytes=64 * 2**20
+            collective_id=0, has_side_effects=True, vmem_limit_bytes=48 * 2**20
         ),
         cost_estimate=pl.CostEstimate(
             flops=entries * 2 * 8 * DEPTH * LANES, bytes_accessed=2**20, transcendentals=entries * 2048
         ),
-    )(waves, shapes, station_list, moveouts)
+    )(*(pltpu.with_memory_space_constraint(a, pltpu.HBM) for a in (waves, shapes, station_list, moveouts)))
 
 
 def solution(mesh):

time: 19.1 us -> 17.8 us (0.932)
  local copies, waits for them, and re-layouts: 1.29 us -> 0.6 us
  Pallas kernels: 17.6 us -> 17.1 us
    unnamed x1, local copies, waits for them, and re-layouts: 1.29 us -> 0.6 us
    pallas_call x1, Pallas kernels: 17.6 us -> 17.1 us  [shards(): pl.pallas_call(functools.partial(kernel, groups, members), out_shape=pltp...]
where the time goes in v3:
time: 17.8 us; the launch traced here: 17.7 us
  Pallas kernels  17.1 us (96%)
  local copies, waits for them, and re-layouts  0.6 us (3%)
    pallas_call x1, Pallas kernels, shards(): pl.pallas_call(functools.partial(kernel, groups, members), out_shape=pltp...  17.1 us
    unnamed x1, local copies, waits for them, and re-layouts  0.6 us

profile of v3, /device:TPU:1, one launch (start us, length us, event | category | flops | bytes accessed | tf_op | source)
XLA Modules:
  0.0 17.7 jit_solution(98204590281555273)
XLA Ops:
  0.0 17.1 %shard_map.46 = f32[2,768]{1,0:T(2,128)S(1)} custom-call(bf16[3,2,1424]{2,1,0:T(2,128)(2,1)} %bitcast.3, bf16[12,3,2,400]{3,2,1,0:T(2,128)(2,1)} %bitcast.2, s32[2,12]{1,0:T(2,128)} %stations_in.1, s32[2,12]{1,0:T(2,128)} %moveouts_in.1), custom_call_target="tpu_custom_call" | custom-call | flops 75497472 | bytes 1048576 | tf_op jit(solution)/shard_map/pallas_call | solution.py:278
  17.1 0.6 %copy.6 = f32[2,768]{1,0:T(2,128)} copy(f32[2,768]{1,0:T(2,128)S(1)} %shard_map.46) | data formatting | bytes 12288
